TPU v7x, 32 devices: a whole 2x2x4 slice. The times are simulated.
32 devices in a mesh: groups: 2 (over y), row: 4 (over z), col: 4 (over x, core).
Axes of the slice: x: 2, y: 2, z: 4, core: 2. Of those that a mesh axis runs over, the one named last changes fastest.
Arguments:
- three_index: bfloat16 [10, 4096, 1024], P('groups', ('row', 'col')), parts along dimension 0, may hold values from -1.1953125 to 1.1953125
- vir_energy: bfloat16 [8192], P(('groups', 'row', 'col')), parts along dimension 0, may hold values from 0.19921875 to 3
- occ_shell: int32 [10], P('groups'), parts along dimension 0, may hold values from 0 to 7
- shell_energy: float32 [16], P('groups'), parts along dimension 0, may hold values from -2 to -0.4
Outputs:
- gamma: float32 [10, 4096, 1024], P('groups', ('row', 'col')), parts along dimension 0
There are 2 independent parts, one for each index of `groups`. A program takes and returns all parts, laid end to end along the dimension named above; each array names one. Nothing has to cross between parts.
All inputs are finite; a program needn't handle non-finite values.
Results may differ from a plain program's by a relative error of at most 0.00072.
Values may be sent and summed in bfloat16 or wider, within the bound.
A program may use at most 320 MiB of HBM per device.

v0:
```python
import jax
import jax.numpy as jnp
from jax import lax
from jax.sharding import PartitionSpec as P


def per_device(three_index, vir_energy, occ_shell, shell_energy):
    levels = jnp.arange(shell_energy.shape[0], dtype=jnp.int32)
    onehot = occ_shell[:, None] == levels[None, :]
    occ_energy = jnp.sum(jnp.where(onehot, shell_energy[None, :], jnp.float32(0.0)), axis=1)
    pair_sum = occ_energy[:, None] + occ_energy[None, :]
    energy_row = vir_energy[None, :]
    own_block, own_energy = (
        lax.all_gather(three_index, "col", axis=1, tiled=True),
        lax.all_gather(energy_row, "col", axis=1, tiled=True),
    )
    own_energy = own_energy[0].astype(jnp.float32)
    partner_all, energy_all = (
        lax.all_gather(three_index, "row", axis=1, tiled=True),
        lax.all_gather(energy_row, "row", axis=1, tiled=True),
    )
    coulomb = jnp.einsum(
        "iaq,jbq->ijab", own_block, partner_all, preferred_element_type=jnp.float32
    )
    denom = (
        pair_sum[:, :, None, None]
        - own_energy[None, None, :, None]
        - energy_all[0].astype(jnp.float32)[None, None, None, :]
    )
    amplitude = ((2.0 * coulomb - jnp.swapaxes(coulomb, 0, 1)) / denom).astype(jnp.bfloat16)
    partial_sum = jnp.einsum(
        "ijab,jbq->iaq", amplitude, partner_all, preferred_element_type=jnp.float32
    )
    return lax.psum_scatter(partial_sum, "col", scatter_dimension=1, tiled=True)


def solution(mesh):
    in_specs = (
        P("groups", ("row", "col"), None),
        P(("groups", "row", "col")),
        P("groups"),
        P("groups"),
    )
    out_specs = P("groups", ("row", "col"), None)
    return jax.shard_map(
        per_device, mesh=mesh, in_specs=in_specs, out_specs=out_specs, check_vma=False
    )
```

profile of v0, /device:TPU:0, one launch (start us, length us, event | category | flops | bytes accessed | tf_op | source)
XLA Modules:
  0.0 598.9 jit_solution(14876251283569036726)
XLA Ops:
  6.5 0.0 all-gather.7.cloned.1.call-start
  6.5 0.7 all-gather.7.cloned.1.call-update
  7.3 0.0 all-gather.9.cloned.1.call-start
  7.3 0.7 all-gather.9.cloned.1.call-update
  8.0 0.0 reduce-scatter.2.cloned.1.call-start
  8.1 0.7 reshape.57
  8.7 12.6 %all-gather.3 = bf16[4,1,256]{2,1,0:T(2,128)(2,1)S(1)} all-gather(bf16[1,1,256]{2,1,0:T(2,128)(2,1)S(1)} %reshape.57), channel_id=3, replica_groups=mesh['groups'=2,'row'=4,'col'=4] {'row'}, dimensions={0}, use_global_device_ids=true | all-gather | bytes 2560 | tf_op jit(solution)/shard_map/all_gather | solution.py:20
  21.3 5.1 all-gather.2
  26.4 0.9 select_reduce_fusion
  27.2 0.1 broadcast_add_fusion
  27.3 0.1 broadcast_subtract_fusion
  27.4 168.2 %all-gather.7.cloned.1.call-done = bf16[5,1024,1024]{2,1,0:T(8,128)(2,1)} async-done(((bf16[5,256,1024]{2,1,0:T(8,128)(2,1)}), bf16[5,1024,1024]{2,1,0:T(8,128)(2,1)}) %all-gather.7.cloned.1.call-update) | async-done | bytes 10485776 | tf_op jit(solution)/shard_map/all_gather | solution.py:19
  195.6 70.0 %all-gather.9.cloned.1.call-done = bf16[5,1024,1024]{2,1,0:T(8,128)(2,1)} async-done(((bf16[5,256,1024]{2,1,0:T(8,128)(2,1)}), bf16[5,1024,1024]{2,1,0:T(8,128)(2,1)}) %all-gather.9.cloned.1.call-update) | async-done | bytes 10485776 | tf_op jit(solution)/shard_map/all_gather | solution.py:14
  265.6 65.0 %fusion.4 = f32[5,1024,5,1024]{3,1,2,0:T(8,128)} fusion(bf16[5,1024,1024]{2,1,0:T(8,128)(2,1)} %all-gather.7.cloned.1.call-done, bf16[5,1024,1024]{2,1,0:T(8,128)(2,1)} %all-gather.9.cloned.1.call-done), kind=kOutput, calls=%fused_computation.5 | convolution fusion | flops 53687091200 | bytes 125829120 | tf_op jit(solution)/shard_map/iaq,jbq->ijab/dot_general | solution.py:22
  330.6 108.5 %fusion.8 = f32[5,1024,1024]{2,1,0:T(8,128)} fusion(bf16[5,1024,1024]{2,1,0:T(8,128)(2,1)} %all-gather.7.cloned.1.call-done, f32[5,1024,5,1024]{3,1,2,0:T(8,128)} %fusion.4, f32[1024]{0:T(1024)S(1)} %bitcast.38, f32[5,5,1024]{2,1,0:T(8,128)S(1)} %broadcast_subtract_fusion), kind=kOutput, calls=%fused_computation.9 | convolution fusion | flops 53818163200 | bytes 136421376 | tf_op jit(solution)/shard_map/ijab,jbq->iaq/dot_general | solution.py:31
  439.1 0.0 reduce-scatter.2.cloned.1.call-update
  439.1 153.3 %reduce-scatter.2.cloned.1.call-done = f32[5,256,1024]{2,1,0:T(8,128)} async-done(((f32[5,1024,1024]{2,1,0:T(8,128)}), f32[5,256,1024]{2,1,0:T(8,128)}) %reduce-scatter.2.cloned.1.call-update) | async-done | bytes 5242896 | tf_op jit(solution)/shard_map/reduce_scatter | solution.py:34
  (2 shorter events, 0.0 us)
Async XLA Ops:
  6.5 189.0 %all-gather.7.cloned.1.call-start = ((), (), s32[]{:S(2)}) async-start(), calls=%async_computation.1 | async-start | bytes 13107200 | tf_op jit(solution)/shard_map/all_gather | solution.py:19
  7.3 258.3 %all-gather.9.cloned.1.call-start = ((), (), s32[]{:S(2)}) async-start(), calls=%async_computation.2 | async-start | bytes 13107200 | tf_op jit(solution)/shard_map/all_gather | solution.py:14
  8.0 584.4 %reduce-scatter.2.cloned.1.call-start = ((), (), s32[]{:S(2)}) async-start(), calls=%async_computation.3 | async-start | bytes 26214400 | tf_op jit(solution)/shard_map/reduce_scatter | solution.py:34
Sparse Core Ops, SparseCore 0:
  8.9 186.6 all-gather.6
  197.1 68.3 all-gather.8
  439.2 153.1 reduce-scatter.1
where the time goes:
time: 599 us
  waiting for transfers between devices  393 us (66%)
  matrix products  173 us (29%)
  blocking collectives  17.7 us (3%)
  between operations  13.1 us (2%)
    all_gather x1, waiting for transfers between devices, per_device(): lax.all_gather(three_index, 'row', axis=1, tiled=True)  168 us
    reduce_scatter x1, waiting for transfers between devices, per_device(): return lax.psum_scatter(partial_sum, 'col', scatter_dimension=1, tiled=True)  153 us
    dot_general x1, matrix products, per_device(): jnp.einsum('ijab,jbq->iaq', amplitude, partner_all, preferred_element_typ...  108 us
    all_gather x1, waiting for transfers between devices, per_device(): lax.all_gather(three_index, 'col', axis=1, tiled=True)  70 us
    dot_general x1, matrix products, per_device(): jnp.einsum('iaq,jbq->ijab', own_block, partner_all, preferred_element_typ...  65 us
    all_gather x1, blocking collectives, per_device(): lax.all_gather(energy_row, 'row', axis=1, tiled=True)  12.6 us
  transfers between devices with their start and end apart: 3, of which 3 were waited for; matrix products, arithmetic and copies ran while one was open for 0% of the time, Pallas kernels for 0%

commit v1 on v0

--- a/solution.py
+++ b/solution.py
@@ -1,13 +1,224 @@
+import functools
+
 import jax
 import jax.numpy as jnp
 from jax import lax
+from jax.experimental import pallas as pl
+from jax.experimental.pallas import tpu as pltpu
 from jax.sharding import PartitionSpec as P
 
-
-def per_device(three_index, vir_energy, occ_shell, shell_energy):
+MESH = pl.DeviceIdType.MESH
+PAD = 16
+UP, DOWN, ACROSS, TWIN = 0, 1, 2, 3
+
+
+def occupied_energies(occ_shell, shell_energy):
     levels = jnp.arange(shell_energy.shape[0], dtype=jnp.int32)
     onehot = occ_shell[:, None] == levels[None, :]
-    occ_energy = jnp.sum(jnp.where(onehot, shell_energy[None, :], jnp.float32(0.0)), axis=1)
+    return jnp.sum(jnp.where(onehot, shell_energy[None, :], jnp.float32(0.0)), axis=1)
+
+
+def gather_and_contract(
+    rows, occ, half, occ_ref, b_ref, vir_row_ref, vir_col_ref, out_ref,
+    held, coulomb, amp, send_sem, recv_sem,
+):
+    r = lax.axis_index("row")
+    c = lax.axis_index("col")
+    k = lax.rem(c, 2)
+    x = c // 2
+    twin_c = 2 * x + (1 - k)
+    across_c = 2 * (1 - x) + k
+    size = occ * half
+    slots = 2 * (rows - 1) + 1
+    has_up, has_down = r + 1 < rows, r > 0
+
+    def chunk_id(row, col, h):
+        return (row * 4 + col) * 2 + h
+
+    def copy(row, other_x, h, way):
+        col = 2 * jnp.where(other_x == 1, 1 - x, x) + k
+        cid = chunk_id(row, col, h)
+        device = {UP: {"row": r + 1}, DOWN: {"row": r - 1}, ACROSS: {"col": across_c}, TWIN: {"col": twin_c}}[way]
+        return pltpu.make_async_remote_copy(
+            src_ref=held.at[cid],
+            dst_ref=held.at[cid],
+            send_sem=send_sem.at[((row * 2 + other_x) * 2 + h) * 4 + way],
+            recv_sem=recv_sem.at[cid],
+            device_id=device,
+            device_id_type=MESH,
+        )
+
+    def arrived(cid):
+        pltpu.make_async_remote_copy(
+            src_ref=held.at[cid],
+            dst_ref=held.at[cid],
+            send_sem=send_sem.at[0],
+            recv_sem=recv_sem.at[cid],
+            device_id={"col": across_c},
+            device_id_type=MESH,
+        ).wait_recv()
+
+    def event(s, j):
+        sign = 2 * lax.rem(j, 2) - 1
+        over_col = j // 2
+        last = s == slots - 1
+        late = jnp.maximum(s - 1, 0)
+        d_row = jnp.where(last, 1, 1 + s // 2)
+        h_row = jnp.where(last, 1, lax.rem(s, 2))
+        d_col = jnp.where(s < 2, 0, 1 + late // 2)
+        h_col = jnp.where(s < 2, s, lax.rem(late, 2))
+        d_col = jnp.where(s == 2, 1, d_col)
+        h_col = jnp.where(s == 2, 0, h_col)
+        d = jnp.where(over_col == 1, d_col, d_row)
+        h = jnp.where(over_col == 1, h_col, h_row)
+        other_x = jnp.where((over_col == 1) | last, 1, 0)
+        row = r + sign * d
+        valid = (row >= 0) & (row < rows) & ((d > 0) | (sign > 0))
+        return row, other_x, d, h, sign, valid
+
+    def own(act):
+        for h in range(2):
+            pl.when(has_up)(lambda h=h: act(copy(r, 0, h, UP)))
+            pl.when(has_down)(lambda h=h: act(copy(r, 0, h, DOWN)))
+            act(copy(r, 0, h, ACROSS))
+            act(copy(r, 0, h, TWIN))
+
+    def onward(row, other_x, d, h, sign, valid, act):
+        line = valid & (other_x == 0)
+        pl.when(line & (sign < 0) & has_up)(lambda: act(copy(row, 0, h, UP)))
+        pl.when(line & (sign > 0) & has_down)(lambda: act(copy(row, 0, h, DOWN)))
+        pl.when(line & ((d > 1) | (h == 0)))(lambda: act(copy(row, 0, h, ACROSS)))
+        pl.when(valid)(lambda: act(copy(row, other_x, h, TWIN)))
+
+    def extra(act):
+        pl.when(has_up)(lambda: act(copy(r, 1, 1, UP)))
+        pl.when(has_down)(lambda: act(copy(r, 1, 1, DOWN)))
+
+    start = lambda desc: desc.start()
+    sent = lambda desc: desc.wait_send()
+
+    mine = chunk_id(r, c, 0)
+    for h in range(2):
+        for i in range(occ):
+            held[mine + h, i * half:(i + 1) * half, :] = b_ref[i, h * half:(h + 1) * half, :]
+        held[mine + h, size:size + PAD, :] = jnp.zeros((PAD, held.shape[-1]), held.dtype)
+        held[mine + h, size:size + PAD, :half] = jnp.broadcast_to(vir_row_ref[h:h + 1, :], (PAD, half))
+
+    barrier = pltpu.get_barrier_semaphore()
+
+    def greet(device):
+        pl.semaphore_signal(barrier, inc=1, device_id=device, device_id_type=MESH)
+
+    pl.when(has_up)(lambda: greet({"row": r + 1}))
+    pl.when(has_down)(lambda: greet({"row": r - 1}))
+    greet({"col": across_c})
+    greet({"col": twin_c})
+    pl.semaphore_wait(barrier, 2 + has_up.astype(jnp.int32) + has_down.astype(jnp.int32))
+
+    own(start)
+    out_ref[...] = jnp.zeros_like(out_ref)
+
+    def contract(cid):
+        vir_b = held[cid, size:size + PAD, :half][:1].astype(jnp.float32)
+        for t in range(2):
+            coulomb[t] = lax.dot_general(
+                held[mine + t, :size, :], held[cid, :size, :],
+                (((1,), (1,)), ((), ())), preferred_element_type=jnp.float32,
+            )
+        for t in range(2):
+            vir_a = vir_col_ref[t * half:(t + 1) * half, :]
+            for i in range(occ):
+                for j in range(i + 1):
+                    inverse = 1.0 / (((occ_ref[i] + occ_ref[j]) - vir_a) - vir_b)
+                    ij = coulomb[t, i * half:(i + 1) * half, j * half:(j + 1) * half]
+                    if i == j:
+                        amp[t, i * half:(i + 1) * half, j * half:(j + 1) * half] = ((2.0 * ij - ij) * inverse).astype(jnp.bfloat16)
+                        continue
+                    ji = coulomb[t, j * half:(j + 1) * half, i * half:(i + 1) * half]
+                    amp[t, i * half:(i + 1) * half, j * half:(j + 1) * half] = ((2.0 * ij - ji) * inverse).astype(jnp.bfloat16)
+                    amp[t, j * half:(j + 1) * half, i * half:(i + 1) * half] = ((2.0 * ji - ij) * inverse).astype(jnp.bfloat16)
+        for t in range(2):
+            out_ref[t] += jnp.dot(amp[t], held[cid, :size, :], preferred_element_type=jnp.float32)
+
+    @pl.loop(0, slots + 1)
+    def _(step):
+        s = step - 1
+        later = jnp.maximum(s, 0)
+
+        @pl.when(step > 0)
+        def _():
+            @pl.loop(0, 4)
+            def _(j):
+                row, other_x, d, h, sign, valid = event(later, j)
+                col = 2 * jnp.where(other_x == 1, 1 - x, x) + k
+
+                @pl.when(valid)
+                def _():
+                    arrived(chunk_id(row, col, h))
+
+                onward(row, other_x, d, h, sign, valid, start)
+
+            pl.when(s == 3)(lambda: extra(start))
+
+        @pl.loop(0, 8)
+        def _(u):
+            row, other_x, _, h, _, valid = event(later, lax.rem(u, 4))
+            first = step == 0
+            core = jnp.where(u // 4 == 0, k, 1 - k)
+            row = jnp.where(first, r, row)
+            other_x = jnp.where(first, 0, other_x)
+            h = jnp.where(first, lax.rem(u, 2), h)
+            go = jnp.where(first, (lax.rem(u, 4) < 2).astype(jnp.int32), valid.astype(jnp.int32)) == 1
+            cid = chunk_id(row, 2 * jnp.where(other_x == 1, 1 - x, x) + core, h)
+
+            @pl.when(go)
+            def _():
+                pl.when(u >= 4)(lambda: arrived(cid))
+                contract(cid)
+
+    own(sent)
+    extra(sent)
+
+    @pl.loop(0, slots)
+    def _(s):
+        @pl.loop(0, 4)
+        def _(j):
+            onward(*event(s, j), sent)
+
+
+def chip_plan(rows, three_index, vir_energy, occ_shell, shell_energy):
+    occ, virtuals, aux = three_index.shape
+    half = virtuals // 2
+    size = occ * half
+    chunks = rows * 4 * 2
+    vmem = pl.BlockSpec(memory_space=pltpu.VMEM)
+    gamma = pl.pallas_call(
+        functools.partial(gather_and_contract, rows, occ, half),
+        out_shape=jax.ShapeDtypeStruct((2, size, aux), jnp.float32),
+        in_specs=[pl.BlockSpec(memory_space=pltpu.SMEM), vmem, vmem, vmem],
+        out_specs=vmem,
+        scratch_shapes=[
+            pltpu.VMEM((chunks, size + PAD, aux), jnp.bfloat16),
+            pltpu.VMEM((2, size, size), jnp.float32),
+            pltpu.VMEM((2, size, size), jnp.bfloat16),
+            pltpu.SemaphoreType.DMA((rows * 2 * 2 * 4,)),
+            pltpu.SemaphoreType.DMA((chunks,)),
+        ],
+        compiler_params=pltpu.CompilerParams(
+            collective_id=0, has_side_effects=True, vmem_limit_bytes=62 * 1024 * 1024
+        ),
+    )(
+        occupied_energies(occ_shell, shell_energy),
+        three_index,
+        vir_energy.reshape(2, half),
+        vir_energy.astype(jnp.float32).reshape(virtuals, 1),
+    )
+    gamma = gamma.reshape(2, occ, half, aux)
+    return jnp.swapaxes(gamma, 0, 1).reshape(occ, virtuals, aux)
+
+
+def gathered_plan(three_index, vir_energy, occ_shell, shell_energy):
+    occ_energy = occupied_energies(occ_shell, shell_energy)
     pair_sum = occ_energy[:, None] + occ_energy[None, :]
     energy_row = vir_energy[None, :]
     own_block, own_energy = (
@@ -35,6 +246,9 @@
 
 
 def solution(mesh):
+    rows, cols = mesh.shape["row"], mesh.shape["col"]
+    fits = rows == 4 and cols == 4
+    plan = functools.partial(chip_plan, rows) if fits else gathered_plan
     in_specs = (
         P("groups", ("row", "col"), None),
         P(("groups", "row", "col")),
@@ -43,5 +257,5 @@
     )
     out_specs = P("groups", ("row", "col"), None)
     return jax.shard_map(
-        per_device, mesh=mesh, in_specs=in_specs, out_specs=out_specs, check_vma=False
-    )
+        plan, mesh=mesh, in_specs=in_specs, out_specs=out_specs, check_vma=False
+    )

time: 599 us -> 241 us (0.40)
  waiting for transfers between devices: 393 us -> 0 us
  Pallas kernels: 0 us -> 232 us
  matrix products: 173 us -> 0 us
  blocking collectives: 17.7 us -> 0 us
  between operations: 13.1 us -> 0.01 us
    all_gather x2 -> x0, waiting for transfers between devices: 238 us -> none  [the longest x1 168 us: per_device(): lax.all_gather(three_index, 'row', axis=1, tiled=True)]
    pallas_call x0 -> x1, Pallas kernels: none -> 232 us  [chip_plan(): pl.pallas_call(functools.partial(gather_and_contract, rows, occ, half), o...]
    dot_general x2 -> x0, matrix products: 173 us -> none  [the longest x1 108 us: per_device(): jnp.einsum('ijab,jbq->iaq', amplitude, partner_all, preferred_element_typ...]
    reduce_scatter x1 -> x0, waiting for transfers between devices: 153 us -> none  [per_device(): return lax.psum_scatter(partial_sum, 'col', scatter_dimension=1, tiled=True)]
    all_gather x2 -> x0, blocking collectives: 17.7 us -> none  [the longest x1 12.6 us: per_device(): lax.all_gather(energy_row, 'row', axis=1, tiled=True)]
  transfers between devices with their start and end apart: 3 -> 0, of which waited for: 3 -> 0; matrix products, arithmetic and copies ran while one was open for 0% -> 0% of each run, Pallas kernels for 0% -> 0%
where the time goes in v1:
time: 241 us; the launch traced here: 240 us
  Pallas kernels  232 us (96%)
  local copies, waits for them, and re-layouts  6.5 us (3%)
    pallas_call x1, Pallas kernels, chip_plan(): pl.pallas_call(functools.partial(gather_and_contract, rows, occ, half), o...  232 us
    transpose x1, local copies, waits for them, and re-layouts, chip_plan(): return jnp.swapaxes(gamma, 0, 1).reshape(occ, virtuals, aux)  5.7 us

profile of v1, /device:TPU:0, one launch (start us, length us, event | category | flops | bytes accessed | tf_op | source)
XLA Modules:
  0.0 240.3 jit_solution(12109840312537526006)
XLA Ops:
  0.0 1.4 select_reduce_fusion.occ_ref
  1.4 0.7 reshape.21
  2.0 0.8 copy.8.vir_col_ref
  2.9 231.7 %shard_map.46 = f32[2,640,1024]{2,1,0:T(8,128)} custom-call(f32[5]{0:T(128)} %select_reduce_fusion.occ_ref, bf16[5,256,1024]{2,1,0:T(8,128)(2,1)} %b_ref.1, bf16[2,128]{1,0:T(2,128)(2,1)} %bitcast.8, f32[256,1]{1,0:T(8,128)} %copy.8.vir_col_ref), custom_call_target="tpu_custom_call" | custom-call | tf_op jit(solution)/shard_map/pallas_call | solution.py:195
  234.6 5.7 %copy.9 = f32[5,2,128,1024]{3,2,1,0:T(8,128)} copy(f32[5,2,128,1024]{3,2,0,1:T(8,128)} %bitcast.6) | data formatting | bytes 10485760 | tf_op jit(solution)/shard_map/transpose | solution.py:217

commit v2 on v1

--- a/solution.py
+++ b/solution.py
@@ -20,7 +20,7 @@
 
 def gather_and_contract(
     rows, occ, half, occ_ref, b_ref, vir_row_ref, vir_col_ref, out_ref,
-    held, coulomb, amp, send_sem, recv_sem,
+    held, held_vir, coulomb, amp, send_sem, recv_sem, send_vir_sem, recv_vir_sem,
 ):
     r = lax.axis_index("row")
     c = lax.axis_index("col")
@@ -39,24 +39,27 @@
         col = 2 * jnp.where(other_x == 1, 1 - x, x) + k
         cid = chunk_id(row, col, h)
         device = {UP: {"row": r + 1}, DOWN: {"row": r - 1}, ACROSS: {"col": across_c}, TWIN: {"col": twin_c}}[way]
-        return pltpu.make_async_remote_copy(
-            src_ref=held.at[cid],
-            dst_ref=held.at[cid],
-            send_sem=send_sem.at[((row * 2 + other_x) * 2 + h) * 4 + way],
-            recv_sem=recv_sem.at[cid],
-            device_id=device,
-            device_id_type=MESH,
-        )
+        return chunk_copies(cid, ((row * 2 + other_x) * 2 + h) * 4 + way, device)
+
+    def chunk_copies(cid, out, device):
+        return [
+            pltpu.make_async_remote_copy(
+                src_ref=ref.at[cid],
+                dst_ref=ref.at[cid],
+                send_sem=sends.at[out],
+                recv_sem=receives.at[cid],
+                device_id=device,
+                device_id_type=MESH,
+            )
+            for ref, sends, receives in (
+                (held_vir, send_vir_sem, recv_vir_sem),
+                (held, send_sem, recv_sem),
+            )
+        ]
 
     def arrived(cid):
-        pltpu.make_async_remote_copy(
-            src_ref=held.at[cid],
-            dst_ref=held.at[cid],
-            send_sem=send_sem.at[0],
-            recv_sem=recv_sem.at[cid],
-            device_id={"col": across_c},
-            device_id_type=MESH,
-        ).wait_recv()
+        for desc in chunk_copies(cid, 0, {"col": across_c}):
+            desc.wait_recv()
 
     def event(s, j):
         sign = 2 * lax.rem(j, 2) - 1
@@ -94,15 +97,20 @@
         pl.when(has_up)(lambda: act(copy(r, 1, 1, UP)))
         pl.when(has_down)(lambda: act(copy(r, 1, 1, DOWN)))
 
-    start = lambda desc: desc.start()
-    sent = lambda desc: desc.wait_send()
+    def start(pair):
+        for desc in pair:
+            desc.start()
+
+    def sent(pair):
+        for desc in pair:
+            desc.wait_send()
+
 
     mine = chunk_id(r, c, 0)
     for h in range(2):
         for i in range(occ):
             held[mine + h, i * half:(i + 1) * half, :] = b_ref[i, h * half:(h + 1) * half, :]
-        held[mine + h, size:size + PAD, :] = jnp.zeros((PAD, held.shape[-1]), held.dtype)
-        held[mine + h, size:size + PAD, :half] = jnp.broadcast_to(vir_row_ref[h:h + 1, :], (PAD, half))
+        held_vir[mine + h] = jnp.broadcast_to(vir_row_ref[h:h + 1, :], (PAD, half))
 
     barrier = pltpu.get_barrier_semaphore()
 
@@ -119,10 +127,10 @@
     out_ref[...] = jnp.zeros_like(out_ref)
 
     def contract(cid):
-        vir_b = held[cid, size:size + PAD, :half][:1].astype(jnp.float32)
+        vir_b = held_vir[cid][:1].astype(jnp.float32)
         for t in range(2):
             coulomb[t] = lax.dot_general(
-                held[mine + t, :size, :], held[cid, :size, :],
+                held[mine + t], held[cid],
                 (((1,), (1,)), ((), ())), preferred_element_type=jnp.float32,
             )
         for t in range(2):
@@ -138,33 +146,40 @@
                     amp[t, i * half:(i + 1) * half, j * half:(j + 1) * half] = ((2.0 * ij - ji) * inverse).astype(jnp.bfloat16)
                     amp[t, j * half:(j + 1) * half, i * half:(i + 1) * half] = ((2.0 * ji - ij) * inverse).astype(jnp.bfloat16)
         for t in range(2):
-            out_ref[t] += jnp.dot(amp[t], held[cid, :size, :], preferred_element_type=jnp.float32)
+            out_ref[t] += jnp.dot(amp[t], held[cid], preferred_element_type=jnp.float32)
+
+    def receive(s, j):
+        row, other_x, d, h, sign, valid = event(s, j)
+        col = 2 * jnp.where(other_x == 1, 1 - x, x) + k
+
+        @pl.when(valid)
+        def _():
+            arrived(chunk_id(row, col, h))
+
+        onward(row, other_x, d, h, sign, valid, start)
 
     @pl.loop(0, slots + 1)
     def _(step):
         s = step - 1
         later = jnp.maximum(s, 0)
 
-        @pl.when(step > 0)
+        @pl.when((step > 0) & (s < slots - 1))
         def _():
             @pl.loop(0, 4)
             def _(j):
-                row, other_x, d, h, sign, valid = event(later, j)
-                col = 2 * jnp.where(other_x == 1, 1 - x, x) + k
-
-                @pl.when(valid)
-                def _():
-                    arrived(chunk_id(row, col, h))
-
-                onward(row, other_x, d, h, sign, valid, start)
+                receive(later, j)
 
             pl.when(s == 3)(lambda: extra(start))
 
         @pl.loop(0, 8)
         def _(u):
-            row, other_x, _, h, _, valid = event(later, lax.rem(u, 4))
             first = step == 0
-            core = jnp.where(u // 4 == 0, k, 1 - k)
+            last = s == slots - 1
+            j = jnp.where(last, lax.rem(u, 2) + 2 * (u // 4), lax.rem(u, 4))
+            twin = jnp.where(last, lax.rem(u // 2, 2), u // 4)
+            pl.when(last & (twin == 0))(lambda: receive(later, j))
+            row, other_x, _, h, _, valid = event(later, j)
+            core = jnp.where(twin == 0, k, 1 - k)
             row = jnp.where(first, r, row)
             other_x = jnp.where(first, 0, other_x)
             h = jnp.where(first, lax.rem(u, 2), h)
@@ -173,7 +188,7 @@
 
             @pl.when(go)
             def _():
-                pl.when(u >= 4)(lambda: arrived(cid))
+                pl.when(twin == 1)(lambda: arrived(cid))
                 contract(cid)
 
     own(sent)
@@ -198,9 +213,12 @@
         in_specs=[pl.BlockSpec(memory_space=pltpu.SMEM), vmem, vmem, vmem],
         out_specs=vmem,
         scratch_shapes=[
-            pltpu.VMEM((chunks, size + PAD, aux), jnp.bfloat16),
+            pltpu.VMEM((chunks, size, aux), jnp.bfloat16),
+            pltpu.VMEM((chunks, PAD, half), jnp.bfloat16),
             pltpu.VMEM((2, size, size), jnp.float32),
             pltpu.VMEM((2, size, size), jnp.bfloat16),
+            pltpu.SemaphoreType.DMA((rows * 2 * 2 * 4,)),
+            pltpu.SemaphoreType.DMA((chunks,)),
             pltpu.SemaphoreType.DMA((rows * 2 * 2 * 4,)),
             pltpu.SemaphoreType.DMA((chunks,)),
         ],

time: 241 us -> 236 us (0.979)
  Pallas kernels: 232 us -> 227 us
    pallas_call x1, Pallas kernels: 232 us -> 227 us  [chip_plan(): pl.pallas_call(functools.partial(gather_and_contract, rows, occ, half), o...]
where the time goes in v2:
time: 236 us
  Pallas kernels  227 us (96%)
  local copies, waits for them, and re-layouts  6.5 us (3%)
    pallas_call x1, Pallas kernels, chip_plan(): pl.pallas_call(functools.partial(gather_and_contract, rows, occ, half), o...  227 us
    transpose x1, local copies, waits for them, and re-layouts, chip_plan(): return jnp.swapaxes(gamma, 0, 1).reshape(occ, virtuals, aux)  5.7 us

profile of v2, /device:TPU:0, one launch (start us, length us, event | category | flops | bytes accessed | tf_op | source)
XLA Modules:
  0.0 236.0 jit_solution(9326716790782503799)
XLA Ops:
  0.0 1.4 select_reduce_fusion.occ_ref
  1.4 0.7 reshape.21
  2.0 0.8 copy.8.vir_col_ref
  2.9 227.4 %shard_map.46 = f32[2,640,1024]{2,1,0:T(8,128)} custom-call(f32[5]{0:T(128)} %select_reduce_fusion.occ_ref, bf16[5,256,1024]{2,1,0:T(8,128)(2,1)} %b_ref.1, bf16[2,128]{1,0:T(2,128)(2,1)} %bitcast.8, f32[256,1]{1,0:T(8,128)} %copy.8.vir_col_ref), custom_call_target="tpu_custom_call" | custom-call | tf_op jit(solution)/shard_map/pallas_call | solution.py:210
  230.3 5.7 %copy.9 = f32[5,2,128,1024]{3,2,1,0:T(8,128)} copy(f32[5,2,128,1024]{3,2,0,1:T(8,128)} %bitcast.6) | data formatting | bytes 10485760 | tf_op jit(solution)/shard_map/transpose | solution.py:235
